TPU v7x, 512 devices: a whole 4x4x16 slice. The times are simulated.
512 devices in a mesh: dp: 8 (over y, core), head: 64 (over x, z).
Axes of the slice: x: 4, y: 4, z: 16, core: 2. Of those that a mesh axis runs over, the one named last changes fastest.
Arguments:
- head_ids: int32 [8, 8192, 8], P('dp', 'head'), may hold values from 0 to 63, as said below
- query_slots: bfloat16 [8, 8192, 8, 128], P('dp', 'head'), may hold values from -300 to 300
- key_slots: bfloat16 [8, 8192, 8, 128], P('dp', 'head'), may hold values from -13 to 13
- value_slots: bfloat16 [8, 8192, 8, 128], P('dp', 'head'), may hold values from -5 to 5
- gate_logits: float32 [8, 8192, 8], P('dp', 'head'), may hold values from -8 to 310
- sink_logits: float32 [64], P('head'), may hold values from 1 to 6
- out_grad: bfloat16 [8, 8192, 8, 128], P('dp', 'head'), may hold values from -6 to 6
Outputs:
- mixed: bfloat16 [8, 8192, 8, 128], P('dp', 'head')
- query_grad: bfloat16 [8, 8192, 8, 128], P('dp', 'head')
- key_grad: bfloat16 [8, 8192, 8, 128], P('dp', 'head')
- value_grad: bfloat16 [8, 8192, 8, 128], P('dp', 'head')
- gate_grad: float32 [8, 8192, 8], P('dp', 'head')
- sink_grad: float32 [64], P('head')
Inputs may be any that keep to these rules, and one draw needn't show every extreme that they name: `head_ids`: each token names 8 different heads. Among the 128 tokens of one device no head is named more than 32 times, and in every group one head is named exactly 32 times by the tokens of every device of that group.
All inputs are finite; a program needn't handle non-finite values.
Results may differ from a plain program's by a relative error of at most 0.023.
Values may be sent and summed in bfloat16 or wider, within the bound.
A program may use at most 64 MiB of HBM per device.

v0:
```python
import math

import jax
import jax.numpy as jnp
from jax import lax
from jax.sharding import PartitionSpec as P

HEADS = 64
BLOCK = 512
SLOT = 32


masked_value = -1e30


def in_one_piece(arrays, axis, split_dim, concat_dim, along):
    widths = [a.shape[along] for a in arrays]
    both = jnp.concatenate(arrays, axis=along)
    filled = lax.all_to_all(both, axis, split_axis=split_dim, concat_axis=concat_dim, tiled=True)
    return tuple(jnp.split(filled, [sum(widths[:k]) for k in range(1, len(widths))], axis=along))


def over_pieces(array, axis):
    parts = lax.all_gather(array, axis)
    return parts.sum(axis=0)


def block_scores(query_tile, key_tile, query_live, key_live, query_offset, key_offset, scale):
    scores = scale * jnp.einsum(
        "qd,kd->qk", query_tile, key_tile, preferred_element_type=jnp.float32
    )
    query_index = query_offset + lax.iota(jnp.int32, query_tile.shape[0])
    key_index = key_offset + lax.iota(jnp.int32, key_tile.shape[0])
    allowed = query_live[:, None] & key_live[None, :] & (key_index[None, :] <= query_index[:, None])
    return (scores, allowed)


def forward_head(query_rows, key_rows, value_rows, live_rows, sink_value, used_blocks, width):
    row_count, head_width = query_rows.shape
    scale = 1.0 / math.sqrt(head_width)

    def forward_query_block(qblock, carry):
        lse_all, out_all = carry
        offset = qblock * width
        query_tile = lax.dynamic_slice_in_dim(query_rows, offset, width, 0)
        query_live = lax.dynamic_slice_in_dim(live_rows, offset, width, 0)

        def tile_at(kblock):
            key_offset = kblock * width
            key_tile = lax.dynamic_slice_in_dim(key_rows, key_offset, width, 0)
            value_tile = lax.dynamic_slice_in_dim(value_rows, key_offset, width, 0)
            key_live = lax.dynamic_slice_in_dim(live_rows, key_offset, width, 0)
            scores, allowed = block_scores(
                query_tile, key_tile, query_live, key_live, offset, key_offset, scale
            )
            return (scores, allowed, value_tile)

        def stat_step(kblock, state):
            run_max, run_sum = state
            scores, allowed, value_tile = tile_at(kblock)
            masked = jnp.where(allowed, scores, masked_value)
            new_max = jnp.maximum(run_max, jnp.max(masked, axis=1))
            new_sum = run_sum * jnp.exp(run_max - new_max) + jnp.sum(
                jnp.where(allowed, jnp.exp(masked - new_max[:, None]), 0.0), axis=1
            )
            return (new_max, new_sum)

        start_state = (jnp.full((width,), sink_value, jnp.float32), jnp.ones((width,), jnp.float32))
        run_max, run_sum = lax.fori_loop(0, qblock + 1, stat_step, start_state)
        row_lse = run_max + jnp.log(run_sum)

        def value_step(kblock, total):
            scores, allowed, value_tile = tile_at(kblock)
            weights = jnp.where(allowed, jnp.exp(scores - row_lse[:, None]), 0.0).astype(
                jnp.bfloat16
            )
            return total + jnp.dot(weights, value_tile, preferred_element_type=jnp.float32)

        total = lax.fori_loop(
            0, qblock + 1, value_step, jnp.zeros((width, head_width), jnp.float32)
        )
        lse_all = lax.dynamic_update_slice_in_dim(lse_all, row_lse, offset, 0)
        out_all = lax.dynamic_update_slice_in_dim(out_all, total.astype(jnp.bfloat16), offset, 0)
        return (lse_all, out_all)

    start_all = (
        jnp.zeros((row_count,), jnp.float32),
        jnp.zeros((row_count, head_width), jnp.bfloat16),
    )
    return lax.fori_loop(0, used_blocks, forward_query_block, start_all)


def backward_head(
    query_rows,
    key_rows,
    value_rows,
    cot_rows,
    head_out,
    lse_all,
    live_rows,
    sink_value,
    used_blocks,
    width,
):
    row_count, head_width = query_rows.shape
    scale = 1.0 / math.sqrt(head_width)
    deltas = jnp.sum(cot_rows.astype(jnp.float32) * head_out.astype(jnp.float32), axis=1)
    sink_term = -jnp.sum(jnp.exp(sink_value - lse_all) * deltas)

    def backward_query_block(qblock, carry):
        qgrad_all, kgrad_acc, vgrad_acc = carry
        offset = qblock * width
        query_tile = lax.dynamic_slice_in_dim(query_rows, offset, width, 0)
        cot_tile = lax.dynamic_slice_in_dim(cot_rows, offset, width, 0)
        lse_tile = lax.dynamic_slice_in_dim(lse_all, offset, width, 0)
        delta_tile = lax.dynamic_slice_in_dim(deltas, offset, width, 0)
        query_live = lax.dynamic_slice_in_dim(live_rows, offset, width, 0)

        def key_step(kblock, inner):
            qgrad_run, kgrad_acc, vgrad_acc = inner
            key_offset = kblock * width
            key_tile = lax.dynamic_slice_in_dim(key_rows, key_offset, width, 0)
            value_tile = lax.dynamic_slice_in_dim(value_rows, key_offset, width, 0)
            key_live = lax.dynamic_slice_in_dim(live_rows, key_offset, width, 0)
            scores, allowed = block_scores(
                query_tile, key_tile, query_live, key_live, offset, key_offset, scale
            )
            probability = jnp.where(allowed, jnp.exp(scores - lse_tile[:, None]), 0.0)
            weights = probability.astype(jnp.bfloat16)
            dprob = jnp.einsum(
                "qd,kd->qk", cot_tile, value_tile, preferred_element_type=jnp.float32
            )
            dscore = (probability * (dprob - delta_tile[:, None])).astype(jnp.bfloat16)
            qgrad_run = qgrad_run + jnp.dot(dscore, key_tile, preferred_element_type=jnp.float32)
            kgrad_part = jnp.einsum(
                "qk,qd->kd", dscore, query_tile, preferred_element_type=jnp.float32
            )
            vgrad_part = jnp.einsum(
                "qk,qd->kd", weights, cot_tile, preferred_element_type=jnp.float32
            )
            kgrad_acc = lax.dynamic_update_slice_in_dim(
                kgrad_acc,
                lax.dynamic_slice_in_dim(kgrad_acc, key_offset, width, 0) + kgrad_part,
                key_offset,
                0,
            )
            vgrad_acc = lax.dynamic_update_slice_in_dim(
                vgrad_acc,
                lax.dynamic_slice_in_dim(vgrad_acc, key_offset, width, 0) + vgrad_part,
                key_offset,
                0,
            )
            return (qgrad_run, kgrad_acc, vgrad_acc)

        start_inner = (jnp.zeros((width, head_width), jnp.float32), kgrad_acc, vgrad_acc)
        qgrad_run, kgrad_acc, vgrad_acc = lax.fori_loop(0, qblock + 1, key_step, start_inner)
        qgrad_all = lax.dynamic_update_slice_in_dim(
            qgrad_all, (scale * qgrad_run).astype(jnp.bfloat16), offset, 0
        )
        return (qgrad_all, kgrad_acc, vgrad_acc)

    start_all = (
        jnp.zeros((row_count, head_width), jnp.bfloat16),
        jnp.zeros((row_count, head_width), jnp.float32),
        jnp.zeros((row_count, head_width), jnp.float32),
    )
    qgrad_all, kgrad_acc, vgrad_acc = lax.fori_loop(0, used_blocks, backward_query_block, start_all)
    return (
        qgrad_all,
        (scale * kgrad_acc).astype(jnp.bfloat16),
        vgrad_acc.astype(jnp.bfloat16),
        sink_term,
    )


def arrange(live_rows, width):
    row_count = live_rows.shape[0]
    return (None, None, row_count // width)


def pick_rows(buffer, head_slot):
    picked = buffer[:, head_slot].reshape(-1, buffer.shape[-1])
    return picked


def restore(row_block, devices):
    return row_block.reshape(devices, -1, row_block.shape[-1])


def per_device(head_ids, query_slots, key_slots, value_slots, gate_logits, sink_logits, out_grad):
    devices = lax.axis_size("head")
    local_heads = HEADS // devices
    selected = head_ids[0]
    token_count, slot_count = selected.shape
    head_width = query_slots.shape[-1]
    matches = (selected[:, :, None] == lax.iota(jnp.int32, HEADS)[None, None, :]).astype(jnp.int32)
    per_token = jnp.sum(matches, axis=1)
    earlier = jnp.cumsum(per_token, axis=0) - per_token
    placing = jnp.sum(matches * earlier[:, None, :], axis=2)
    target = (selected * SLOT + placing).reshape(-1)
    buffer_rows = HEADS * SLOT

    def spread_out(flat_rows):
        filled_rows = (
            jnp.zeros((buffer_rows, flat_rows.shape[-1]), flat_rows.dtype).at[target].set(flat_rows)
        )
        return filled_rows.reshape(devices, local_heads, SLOT, flat_rows.shape[-1])

    def collect(buffer):
        return buffer.reshape(buffer_rows, buffer.shape[-1])[target].reshape(
            token_count, slot_count, buffer.shape[-1]
        )

    gate_probs = jax.nn.softmax(gate_logits[0], axis=-1)
    cotangent = (gate_probs[:, :, None] * out_grad[0].astype(jnp.float32)).astype(jnp.bfloat16)
    send_query = spread_out(query_slots[0].reshape(-1, head_width))
    send_key = spread_out(key_slots[0].reshape(-1, head_width))
    send_value = spread_out(value_slots[0].reshape(-1, head_width))
    send_cot = spread_out(cotangent.reshape(-1, head_width))
    filled = (
        jnp.zeros((buffer_rows,), jnp.bfloat16)
        .at[target]
        .set(jnp.ones((), jnp.bfloat16))
        .reshape(devices, local_heads, SLOT)
    )
    out_list, qgrad_list, kgrad_list, vgrad_list, sink_list = ([], [], [], [], [])
    recv_query, recv_key, recv_value, recv_cot, recv_fill = (
        lax.all_to_all(send_query, "head", split_axis=0, concat_axis=0, tiled=True),
        lax.all_to_all(send_key, "head", split_axis=0, concat_axis=0, tiled=True),
        lax.all_to_all(send_value, "head", split_axis=0, concat_axis=0, tiled=True),
        lax.all_to_all(send_cot, "head", split_axis=0, concat_axis=0, tiled=True),
        lax.all_to_all(filled, "head", split_axis=0, concat_axis=0, tiled=True),
    )
    live_rows = recv_fill[:, 0].reshape(-1) > 0
    gather_order, landing, used_blocks = arrange(live_rows, BLOCK)
    live_use = live_rows
    pieces = (pick_rows(recv_query, 0), pick_rows(recv_key, 0), pick_rows(recv_value, 0))
    pieces, live_use, gather_order, landing, used_blocks = (
        pieces,
        live_use,
        gather_order,
        landing,
        used_blocks,
    )
    row_lse, head_out = forward_head(
        pieces[0], pieces[1], pieces[2], live_use, sink_logits[0], used_blocks, BLOCK
    )
    cot_rows = pick_rows(recv_cot, 0)
    qgrad, kgrad, vgrad, sink_term = backward_head(
        pieces[0],
        pieces[1],
        pieces[2],
        cot_rows,
        head_out,
        row_lse,
        live_use,
        sink_logits[0],
        used_blocks,
        BLOCK,
    )
    out_list.append(restore(head_out, devices))
    qgrad_list.append(restore(qgrad, devices))
    kgrad_list.append(restore(kgrad, devices))
    vgrad_list.append(restore(vgrad, devices))
    sink_list.append(sink_term)
    back_out, back_qgrad, back_kgrad, back_vgrad = in_one_piece(
        (
            jnp.stack(out_list, axis=1),
            jnp.stack(qgrad_list, axis=1),
            jnp.stack(kgrad_list, axis=1),
            jnp.stack(vgrad_list, axis=1),
        ),
        "head",
        0,
        0,
        1,
    )
    sink_grad = over_pieces(jnp.stack(sink_list), "dp")
    token_out = collect(back_out).astype(jnp.float32)
    mixed = (gate_probs[:, :, None] * token_out).astype(jnp.bfloat16)
    gate_sum = jnp.sum(out_grad[0].astype(jnp.float32) * token_out, axis=-1)
    gate_grad = gate_probs * (gate_sum - jnp.sum(gate_probs * gate_sum, axis=-1, keepdims=True))
    return (
        mixed[None],
        collect(back_qgrad)[None],
        collect(back_kgrad)[None],
        collect(back_vgrad)[None],
        gate_grad[None],
        sink_grad,
    )


def solution(mesh):
    placed = (
        P("dp", "head", None),
        P("dp", "head", None, None),
        P("dp", "head", None, None),
        P("dp", "head", None, None),
        P("dp", "head", None),
        P("head"),
        P("dp", "head", None, None),
    )
    return jax.shard_map(
        per_device,
        mesh=mesh,
        in_specs=placed,
        out_specs=(
            P("dp", "head", None, None),
            P("dp", "head", None, None),
            P("dp", "head", None, None),
            P("dp", "head", None, None),
            P("dp", "head", None),
            P("head"),
        ),
        check_vma=False,
    )
```

profile of v0, /device:TPU:6, one launch (start us, length us, event | category | flops | bytes accessed | tf_op | source)
XLA Modules:
  0.0 368.5 jit_solution(15139266547399132379)
XLA Ops:
  3.7 7.6 %scatter_custom_fusion.1 = bf16[2048]{0:T(1024)(128)(2,1)S(1)} fusion(s32[1024]{0:T(1024)S(1)} %bitcast.142, bf16[1024]{0:T(1024)(128)(2,1)S(1)} %broadcast.186, bf16[]{:T(256)} %constant.140.clone.1), kind=kCustom, calls=%fused_computation.114 | custom fusion | bytes 4098 | tf_op jit(solution)/shard_map/scatter | solution.py:223
  12.0 18.8 %all-to-all-start.1 = ((bf16[64,1,32]{2,1,0:T(2,128)(2,1)}), bf16[64,1,32]{2,1,0:T(2,128)(2,1)S(1)}, u32[]{:S(2)}, u32[]{:S(2)}) async-start(bf16[64,1,32]{2,1,0:T(2,128)(2,1)} %reshape.314), calls=%async_computation.1 | async-start | bytes 65536 | tf_op jit(solution)/shard_map/all_to_all | solution.py:232
  30.8 4.0 %scatter_custom_fusion = bf16[2048,128]{1,0:T(8,128)(2,1)} fusion(s32[1024]{0:T(1024)S(1)} %bitcast.143, bf16[1,128,8,128]{3,2,1,0:T(8,128)(2,1)S(1)} %copy-done, bf16[]{:T(256)} %constant.140.clone.1), kind=kCustom, calls=%fused_computation.92 | custom fusion | bytes 786434 | tf_op jit(solution)/shard_map/scatter | solution.py:205
  34.8 8.5 %all-to-all-done.1 = bf16[64,1,32]{2,1,0:T(2,128)(2,1)S(1)} async-done(((bf16[64,1,32]{2,1,0:T(2,128)(2,1)}), bf16[64,1,32]{2,1,0:T(2,128)(2,1)S(1)}, u32[]{:S(2)}, u32[]{:S(2)}) %all-to-all-start.1) | async-done | bytes 4128 | tf_op jit(solution)/shard_map/all_to_all | solution.py:232
  43.2 6.6 %all-to-all-start = ((bf16[64,1,32,128]{3,2,1,0:T(8,128)(2,1)}), bf16[64,1,32,128]{3,2,1,0:T(8,128)(2,1)S(1)}, u32[]{:S(2)}, u32[]{:S(2)}) async-start(bf16[64,1,32,128]{3,2,1,0:T(8,128)(2,1)} %bitcast.9), calls=%async_computation | async-start | bytes 1048576 | tf_op jit(solution)/shard_map/all_to_all | solution.py:228
  49.9 4.0 %scatter_custom_fusion.2 = bf16[2048,128]{1,0:T(8,128)(2,1)} fusion(s32[1024]{0:T(1024)S(1)} %bitcast.144, bf16[1,128,8,128]{3,2,1,0:T(8,128)(2,1)S(1)} %copy-done.8, bf16[]{:T(256)} %constant.140.clone.1), kind=kCustom, calls=%fused_computation.90 | custom fusion | bytes 786434 | tf_op jit(solution)/shard_map/scatter | solution.py:205
  53.9 26.5 %all-to-all-done = bf16[64,1,32,128]{3,2,1,0:T(8,128)(2,1)S(1)} async-done(((bf16[64,1,32,128]{3,2,1,0:T(8,128)(2,1)}), bf16[64,1,32,128]{3,2,1,0:T(8,128)(2,1)S(1)}, u32[]{:S(2)}, u32[]{:S(2)}) %all-to-all-start) | async-done | bytes 524320 | tf_op jit(solution)/shard_map/all_to_all | solution.py:228
  80.5 7.2 %all-to-all-start.2 = ((bf16[64,1,32,128]{3,2,1,0:T(8,128)(2,1)}), bf16[64,1,32,128]{3,2,1,0:T(8,128)(2,1)S(1)}, u32[]{:S(2)}, u32[]{:S(2)}) async-start(bf16[64,1,32,128]{3,2,1,0:T(8,128)(2,1)} %bitcast.12), calls=%async_computation.2 | async-start | bytes 1048576 | tf_op jit(solution)/shard_map/all_to_all | solution.py:229
  87.7 4.0 %scatter_custom_fusion.3 = bf16[2048,128]{1,0:T(8,128)(2,1)} fusion(s32[1024]{0:T(1024)S(1)} %bitcast.145, bf16[1,128,8,128]{3,2,1,0:T(8,128)(2,1)S(1)} %copy-done.9, bf16[]{:T(256)} %constant.140.clone.1), kind=kCustom, calls=%fused_computation.88 | custom fusion | bytes 786434 | tf_op jit(solution)/shard_map/scatter | solution.py:205
  91.7 26.7 %all-to-all-done.2 = bf16[64,1,32,128]{3,2,1,0:T(8,128)(2,1)S(1)} async-done(((bf16[64,1,32,128]{3,2,1,0:T(8,128)(2,1)}), bf16[64,1,32,128]{3,2,1,0:T(8,128)(2,1)S(1)}, u32[]{:S(2)}, u32[]{:S(2)}) %all-to-all-start.2) | async-done | bytes 524320 | tf_op jit(solution)/shard_map/all_to_all | solution.py:229
  118.4 7.4 %all-to-all-start.3 = ((bf16[64,1,32,128]{3,2,1,0:T(8,128)(2,1)}), bf16[64,1,32,128]{3,2,1,0:T(8,128)(2,1)}, u32[]{:S(2)}, u32[]{:S(2)}) async-start(bf16[64,1,32,128]{3,2,1,0:T(8,128)(2,1)} %bitcast.15), calls=%async_computation.3 | async-start | bytes 1048576 | tf_op jit(solution)/shard_map/all_to_all | solution.py:230
  126.6 4.5 %scatter_custom_fusion.4 = bf16[2048,128]{1,0:T(8,128)(2,1)} fusion(s32[1024]{0:T(1024)S(1)} %bitcast.146, bf16[1,128,8,128]{3,2,1,0:T(8,128)(2,1)S(1)} %copy-done.6, f32[1024]{0:T(1024)S(1)} %exponential_divide_fusion, bf16[]{:T(256)} %constant.140.clone.1), kind=kCustom, calls=%fused_computation.87 | custom fusion | flops 393216 | bytes 790530 | tf_op jit(solution)/shard_map/scatter | solution.py:205
  131.4 25.2 %all-to-all-done.3 = bf16[64,1,32,128]{3,2,1,0:T(8,128)(2,1)} async-done(((bf16[64,1,32,128]{3,2,1,0:T(8,128)(2,1)}), bf16[64,1,32,128]{3,2,1,0:T(8,128)(2,1)}, u32[]{:S(2)}, u32[]{:S(2)}) %all-to-all-start.3) | async-done | bytes 524320 | tf_op jit(solution)/shard_map/all_to_all | solution.py:230
  156.5 7.2 %all-to-all-start.4 = ((bf16[64,1,32,128]{3,2,1,0:T(8,128)(2,1)}), bf16[64,1,32,128]{3,2,1,0:T(8,128)(2,1)S(1)}, u32[]{:S(2)}, u32[]{:S(2)}) async-start(bf16[64,1,32,128]{3,2,1,0:T(8,128)(2,1)} %bitcast.19), calls=%async_computation.4 | async-start | bytes 1048576 | tf_op jit(solution)/shard_map/all_to_all | solution.py:231
  163.8 31.6 %while.114 = (s32[]{:T(128)}, f32[2048]{0:T(1024)S(1)}, bf16[2048,128]{1,0:T(8,128)(2,1)S(1)}, f32[]{:T(128)}, bf16[2048,128]{1,0:T(8,128)(2,1)S(1)}, /*index=5*...) while((s32[]{:T(128)}, f32[2048]{0:T(1024)S(1)}, ...), condition=%wide.region_16.17_spmd, body=%wide.region_9.16_spmd.sunk | while | flops 206442000 | bytes 4263793 | solution.py:90
  165.8 1.8 while.118
  165.9 1.7 fusion.125
  168.4 1.9 while.117
  170.5 3.6 while.118
  170.6 1.7 fusion.125
  172.4 1.7 fusion.125
  174.9 2.9 while.117
  178.0 5.4 %while.118 = (s32[]{:T(128)}, f32[512,128]{1,0:T(8,128)S(1)}, s32[]{:T(128)}, pred[512]{0:T(512)(128)(4,1)S(1)}, pred[2048]{0:T(1024)(128)(4,1)S(1)}, /*index=5*...) while((s32[]{:T(128)}, f32[512,128]{1,0:T(8,128)S(1)}, ...), condition=%wide.region_15.15_spmd, body=%wide.region_14.14_spmd.sunk | while | flops 136119296 | bytes 931007 | solution.py:79
  178.1 1.7 fusion.125
  179.9 1.7 fusion.125
  181.6 1.7 fusion.125
  184.2 3.9 %while.117 = (s32[]{:T(128)}, f32[512]{0:T(512)S(1)}, f32[512]{0:T(512)S(1)}, s32[]{:T(128)}, pred[512]{0:T(512)(128)(4,1)S(1)}, /*index=5*/pred[2048]{0:T(1024)...) while((s32[]{:T(128)}, f32[512]{0:T(512)S(1)}, ...), condition=%wide.region_13.13_spmd, body=%wide.region_10.12_spmd.sunk | while | flops 70256648 | bytes 2401467 | solution.py:69
  188.2 7.2 %while.118 = (s32[]{:T(128)}, f32[512,128]{1,0:T(8,128)S(1)}, s32[]{:T(128)}, pred[512]{0:T(512)(128)(4,1)S(1)}, pred[2048]{0:T(1024)(128)(4,1)S(1)}, /*index=5*...) while((s32[]{:T(128)}, f32[512,128]{1,0:T(8,128)S(1)}, ...), condition=%wide.region_15.15_spmd, body=%wide.region_14.14_spmd.sunk | while | flops 136119296 | bytes 931007 | solution.py:79
  188.3 1.7 fusion.125
  190.1 1.7 fusion.125
  191.9 1.7 fusion.125
  193.7 1.7 fusion.125
  197.6 35.6 %while.116 = (s32[]{:T(128)}, bf16[2048,128]{1,0:T(8,128)(2,1)}, f32[2048,128]{1,0:T(8,128)S(1)}, f32[2048,128]{1,0:T(8,128)S(1)}, bf16[2048,128]{1,0:T(8,128)(2...) while((s32[]{:T(128)}, bf16[2048,128]{1,0:T(8,128)(2,1)}, ...), condition=%wide.region_22.23_spmd, body=%wide.region_19.22_spmd.sunk | while | flops 338494464 | bytes 8412806 | solution.py:167
  198.8 2.8 while.119
  203.5 5.6 %while.119 = (s32[]{:T(128)}, f32[512,128]{1,0:T(8,128)S(1)}, f32[2048,128]{1,0:T(8,128)S(1)}, f32[2048,128]{1,0:T(8,128)S(1)}, s32[]{:T(128)}, /*index=5*/pred[...) while((s32[]{:T(128)}, f32[512,128]{1,0:T(8,128)S(1)}, ...), condition=%wide.region_21.21_spmd, body=%wide.region_20.20_spmd.sunk | while | flops 338363392 | bytes 7223539 | solution.py:156
  211.0 8.4 %while.119 = (s32[]{:T(128)}, f32[512,128]{1,0:T(8,128)S(1)}, f32[2048,128]{1,0:T(8,128)S(1)}, f32[2048,128]{1,0:T(8,128)S(1)}, s32[]{:T(128)}, /*index=5*/pred[...) while((s32[]{:T(128)}, f32[512,128]{1,0:T(8,128)S(1)}, ...), condition=%wide.region_21.21_spmd, body=%wide.region_20.20_spmd.sunk | while | flops 338363392 | bytes 7223539 | solution.py:156
  217.2 1.2 fusion.117
  221.3 11.2 %while.119 = (s32[]{:T(128)}, f32[512,128]{1,0:T(8,128)S(1)}, f32[2048,128]{1,0:T(8,128)S(1)}, f32[2048,128]{1,0:T(8,128)S(1)}, s32[]{:T(128)}, /*index=5*/pred[...) while((s32[]{:T(128)}, f32[512,128]{1,0:T(8,128)S(1)}, ...), condition=%wide.region_21.21_spmd, body=%wide.region_20.20_spmd.sunk | while | flops 338363392 | bytes 7223539 | solution.py:156
  234.3 1.5 pad_maximum_fusion
  235.9 15.3 %all-to-all-start.5 = ((bf16[64,4,32,128]{3,2,1,0:T(8,128)(2,1)}), bf16[64,4,32,128]{3,2,1,0:T(8,128)(2,1)}, u32[]{:S(2)}, u32[]{:S(2)}) async-start(bf16[64,4,32,128]{3,2,1,0:T(8,128)(2,1)} %pad_maximum_fusion), calls=%async_computation.5 | async-start | bytes 4194304 | tf_op jit(solution)/shard_map/all_to_all | solution.py:19
  251.9 1.3 dynamic-slice
  255.2 14.2 %all-reduce = f32[8]{0:T(128)S(1)} all-reduce(f32[8]{0:T(128)S(1)} %dynamic-update-slice), channel_id=1, replica_groups=mesh['dp'=8,'head'=64] {'dp'}, use_global_device_ids=true, to_apply=%add | all-reduce | flops 8 | bytes 64
  269.9 78.5 %all-to-all-done.5 = bf16[64,4,32,128]{3,2,1,0:T(8,128)(2,1)} async-done(((bf16[64,4,32,128]{3,2,1,0:T(8,128)(2,1)}), bf16[64,4,32,128]{3,2,1,0:T(8,128)(2,1)}, u32[]{:S(2)}, u32[]{:S(2)}) %all-to-all-start.5) | async-done | bytes 2097184 | tf_op jit(solution)/shard_map/all_to_all | solution.py:19
  348.4 1.9 fusion.73
  350.4 3.2 gather_fusion
  354.1 4.3 %gather_fusion.1 = bf16[1024,128]{1,0:T(8,128)(2,1)} fusion(bf16[2048,128]{1,0:T(8,128)(2,1)S(1)} %bitcast.129, s32[1024]{0:T(1024)S(1)} %broadcast_clamp_fusion), kind=kCustom, calls=%fused_computation.1 | custom fusion | bytes 528384 | tf_op jit(solution)/shard_map/gather | solution.py:210
  358.4 4.3 %gather_fusion.2 = bf16[1024,128]{1,0:T(8,128)(2,1)} fusion(bf16[2048,128]{1,0:T(8,128)(2,1)S(1)} %bitcast.128, s32[1024]{0:T(1024)S(1)} %broadcast_clamp_fusion), kind=kCustom, calls=%fused_computation.2 | custom fusion | bytes 528384 | tf_op jit(solution)/shard_map/gather | solution.py:210
  362.7 4.3 %gather_fusion.3 = bf16[1024,128]{1,0:T(8,128)(2,1)} fusion(bf16[2048,128]{1,0:T(8,128)(2,1)S(1)} %bitcast.127, s32[1024]{0:T(1024)S(1)} %broadcast_clamp_fusion), kind=kCustom, calls=%fused_computation.3 | custom fusion | bytes 528384 | tf_op jit(solution)/shard_map/gather | solution.py:210
  (278 shorter events, 60.4 us)
Async XLA Ops:
  0.6 30.1 %copy-start = (bf16[1,128,8,128]{3,2,1,0:T(8,128)(2,1)S(1)}, bf16[1,128,8,128]{3,2,1,0:T(8,128)(2,1)}, u32[]{:S(2)}) copy-start(bf16[1,128,8,128]{3,2,1,0:T(8,128)(2,1)} %param.18) | copy-start | bytes 786436
  0.6 49.2 %copy-start.8 = (bf16[1,128,8,128]{3,2,1,0:T(8,128)(2,1)S(1)}, bf16[1,128,8,128]{3,2,1,0:T(8,128)(2,1)}, u32[]{:S(2)}) copy-start(bf16[1,128,8,128]{3,2,1,0:T(8,128)(2,1)} %param.19) | copy-start | bytes 786436
  2.4 85.3 %copy-start.9 = (bf16[1,128,8,128]{3,2,1,0:T(8,128)(2,1)S(1)}, bf16[1,128,8,128]{3,2,1,0:T(8,128)(2,1)}, u32[]{:S(2)}) copy-start(bf16[1,128,8,128]{3,2,1,0:T(8,128)(2,1)} %param.20) | copy-start | bytes 786436
  12.0 31.3 %all-to-all-start.1 = ((bf16[64,1,32]{2,1,0:T(2,128)(2,1)}), bf16[64,1,32]{2,1,0:T(2,128)(2,1)S(1)}, u32[]{:S(2)}, u32[]{:S(2)}) async-start(bf16[64,1,32]{2,1,0:T(2,128)(2,1)} %reshape.314), calls=%async_computation.1 | async-start | bytes 65536 | tf_op jit(solution)/shard_map/all_to_all | solution.py:232
  43.2 37.2 %all-to-all-start = ((bf16[64,1,32,128]{3,2,1,0:T(8,128)(2,1)}), bf16[64,1,32,128]{3,2,1,0:T(8,128)(2,1)S(1)}, u32[]{:S(2)}, u32[]{:S(2)}) async-start(bf16[64,1,32,128]{3,2,1,0:T(8,128)(2,1)} %bitcast.9), calls=%async_computation | async-start | bytes 1048576 | tf_op jit(solution)/shard_map/all_to_all | solution.py:228
  49.9 76.0 %copy-start.10 = (f32[1,128,8]{1,2,0:T(8,128)S(1)}, f32[1,128,8]{1,2,0:T(8,128)}, u32[]{:S(2)}) copy-start(f32[1,128,8]{1,2,0:T(8,128)} %param.21) | copy-start | bytes 12292
  49.9 76.7 %copy-start.6 = (bf16[1,128,8,128]{3,2,1,0:T(8,128)(2,1)S(1)}, bf16[1,128,8,128]{3,2,1,0:T(8,128)(2,1)}, u32[]{:S(2)}) copy-start(bf16[1,128,8,128]{3,2,1,0:T(8,128)(2,1)} %param.23) | copy-start | bytes 786436
  80.5 38.0 %all-to-all-start.2 = ((bf16[64,1,32,128]{3,2,1,0:T(8,128)(2,1)}), bf16[64,1,32,128]{3,2,1,0:T(8,128)(2,1)S(1)}, u32[]{:S(2)}, u32[]{:S(2)}) async-start(bf16[64,1,32,128]{3,2,1,0:T(8,128)(2,1)} %bitcast.12), calls=%async_computation.2 | async-start | bytes 1048576 | tf_op jit(solution)/shard_map/all_to_all | solution.py:229
  118.4 38.1 %all-to-all-start.3 = ((bf16[64,1,32,128]{3,2,1,0:T(8,128)(2,1)}), bf16[64,1,32,128]{3,2,1,0:T(8,128)(2,1)}, u32[]{:S(2)}, u32[]{:S(2)}) async-start(bf16[64,1,32,128]{3,2,1,0:T(8,128)(2,1)} %bitcast.15), calls=%async_computation.3 | async-start | bytes 1048576 | tf_op jit(solution)/shard_map/all_to_all | solution.py:230
  156.5 38.9 %all-to-all-start.4 = ((bf16[64,1,32,128]{3,2,1,0:T(8,128)(2,1)}), bf16[64,1,32,128]{3,2,1,0:T(8,128)(2,1)S(1)}, u32[]{:S(2)}, u32[]{:S(2)}) async-start(bf16[64,1,32,128]{3,2,1,0:T(8,128)(2,1)} %bitcast.19), calls=%async_computation.4 | async-start | bytes 1048576 | tf_op jit(solution)/shard_map/all_to_all | solution.py:231
  195.4 1.0 copy-start.3
  195.4 1.1 copy-start.1
  195.4 1.0 copy-start.2
  233.2 1.0 copy-start.4
  233.2 1.2 copy-start.5
  235.9 112.5 %all-to-all-start.5 = ((bf16[64,4,32,128]{3,2,1,0:T(8,128)(2,1)}), bf16[64,4,32,128]{3,2,1,0:T(8,128)(2,1)}, u32[]{:S(2)}, u32[]{:S(2)}) async-start(bf16[64,4,32,128]{3,2,1,0:T(8,128)(2,1)} %pad_maximum_fusion), calls=%async_computation.5 | async-start | bytes 4194304 | tf_op jit(solution)/shard_map/all_to_all | solution.py:19
  350.4 3.2 copy-start.7
where the time goes:
time: 370 us; the launch traced here: 369 us
  waiting for transfers between devices  165 us (45%)
  starting transfers between devices  62.6 us (17%)
  local copies, waits for them, and re-layouts  55 us (15%)
  matrix products  47.3 us (13%)
  other arithmetic  19.9 us (5%)
  blocking collectives  14.2 us (4%)
    all_to_all x1, waiting for transfers between devices, in_one_piece(): lax.all_to_all(both, axis, split_axis=split_dim, concat_axis=concat_dim,...  78.5 us
    all_to_all x1, waiting for transfers between devices, per_device(): lax.all_to_all(send_key, 'head', split_axis=0, concat_axis=0, tiled=True)  26.7 us
    all_to_all x1, waiting for transfers between devices, per_device(): lax.all_to_all(send_query, 'head', split_axis=0, concat_axis=0, tiled=True)  26.5 us
    all_to_all x1, waiting for transfers between devices, per_device(): lax.all_to_all(send_value, 'head', split_axis=0, concat_axis=0, tiled=True)  25.2 us
    all_to_all x1, starting transfers between devices, per_device(): lax.all_to_all(filled, 'head', split_axis=0, concat_axis=0, tiled=True)  18.8 us
    dot_general x10, matrix products, value_step(): jnp.dot(weights, value_tile, preferred_element_type=jnp.float32)  16.7 us
    gather x4, local copies, waits for them, and re-layouts, collect(): buffer.reshape(buffer_rows, buffer.shape[-1])[target]  16.1 us
    all_to_all x1, starting transfers between devices, in_one_piece(): lax.all_to_all(both, axis, split_axis=split_dim, concat_axis=concat_dim,...  15.3 us
  transfers between devices with their start and end apart: 6, of which 5 were waited for; matrix products, arithmetic and copies ran while one was open for 14% of the time, Pallas kernels for 0%

commit v1 on v0

v1 whole, which is shorter than its diff:
```python
import math

import jax
import jax.numpy as jnp
from jax import lax
from jax.experimental import pallas as pl
from jax.experimental.pallas import tpu as pltpu
from jax.sharding import PartitionSpec as P

HEADS = 64
SLOT = 32
DEAD = 2.0**100
MASKED = -1e30
BLOCK = 256
MESH = pl.DeviceIdType.MESH
f32, bf16 = jnp.float32, jnp.bfloat16


def dot(a, b, dims=((1,), (0,))):
    return lax.dot_general(a, b, (dims, ((), ())), preferred_element_type=f32)


def iota(shape, dim):
    return lax.broadcasted_iota(jnp.int32, shape, dim)


def one_hot(mask):
    return jnp.where(mask, 1.0, 0.0).astype(bf16)


def block_at(n):
    return pl.ds(pl.multiple_of(n * BLOCK, BLOCK), BLOCK)


def places(ids, rows):
    slots, tokens = ids.shape
    head = iota((HEADS, tokens), 0)
    named = [head == ids[j : j + 1] for j in range(slots)]
    count = sum(jnp.where(mask, 1.0, 0.0) for mask in named).astype(bf16)
    earlier = dot(count, one_hot(iota((tokens, tokens), 0) < iota((tokens, tokens), 1)))
    rank = jnp.concatenate(
        [jnp.sum(jnp.where(mask, earlier, 0.0), axis=0, keepdims=True) for mask in named], axis=0
    )
    spread = one_hot(iota((tokens, rows), 0) == iota((tokens, rows), 1) // slots)
    place = dot(ids.astype(f32).astype(bf16), spread) * SLOT + dot(rank.astype(bf16), spread)
    mine = iota((slots, rows), 0) == iota((slots, rows), 1) % slots
    return jnp.sum(jnp.where(mine, place, 0.0), axis=0, keepdims=True).astype(jnp.int32)


def pack(place, wide, send):
    rows, width = wide.shape[0], wide.shape[1] // 4
    ones = jnp.ones((rows, width), bf16)

    def chunk(c, carry):
        slot = c * BLOCK + iota((BLOCK, rows), 0)
        pick = one_hot(slot == place)
        moved = dot(pick, wide[...])
        live = dot(pick, ones)
        for a in range(4):
            part = moved[:, a * width : (a + 1) * width]
            if a == 1:
                part = jnp.where((live < 0.5) & (iota((BLOCK, width), 1) == 0), DEAD, part)
            send[a, block_at(c), :] = part.astype(bf16)
        return carry

    lax.fori_loop(0, send.shape[1] // BLOCK, chunk, 0)


def forward(recv, sink, out, probs, strip, bias, sink_share, factor):
    blocks = recv.shape[1] // BLOCK
    half = recv.shape[2]
    first = one_hot(iota((8, half), 1) == 0)

    def bias_block(j, carry):
        mark = dot(first, recv[1, block_at(j), :], ((1,), (1,)))
        bias[j] = jnp.where(mark > 0.5 * DEAD, MASKED, 0.0)
        return carry

    lax.fori_loop(0, blocks, bias_block, 0)
    causal = iota((BLOCK, BLOCK), 1) <= iota((BLOCK, BLOCK), 0)

    def query_block(i, carry):
        query = recv[0, block_at(i), :]

        def scores(j):
            raw = dot(query, recv[1, block_at(j), :], ((1,), (1,))) * factor
            return jnp.where(bias[j][0:1] < 0.0, MASKED, raw)

        def halves(tile):
            return [tile[:, n * half : (n + 1) * half] for n in range(BLOCK // half)]

        def score_step(j, top):
            tile = scores(j)
            strip[j] = tile
            for part in halves(tile):
                top = jnp.maximum(top, part)
            return top

        top = lax.fori_loop(0, i, score_step, jnp.full((BLOCK, half), sink, f32))
        tile = jnp.where(causal, scores(i), MASKED)
        strip[i] = tile
        for part in halves(tile):
            top = jnp.maximum(top, part)
        top = jnp.max(top, axis=1, keepdims=True)

        def sum_step(j, total):
            weight = jnp.exp2(strip[j] - top)
            strip[j] = weight
            for part in halves(weight):
                total = total + part
            return total

        zero = jnp.zeros((BLOCK, half), f32)
        total = lax.fori_loop(0, i + 1, sum_step, zero)
        sink_part = jnp.exp2(sink - top)
        scale = 1.0 / (jnp.sum(total, axis=1, keepdims=True) + sink_part)

        def value_step(j, acc):
            weight = (strip[j] * scale).astype(bf16)
            probs[i, j] = weight
            return acc + dot(weight, recv[2, block_at(j), :])

        acc = lax.fori_loop(0, i + 1, value_step, zero)
        out[0, block_at(i), :] = acc.astype(bf16)
        sink_share[block_at(i), :] = jnp.broadcast_to(sink_part * scale, (BLOCK, half))
        return carry

    lax.fori_loop(0, blocks, query_block, 0)


def backward(recv, out, probs, sink_share, kgrad, vgrad, root):
    blocks = recv.shape[1] // BLOCK
    width = recv.shape[2]
    kgrad[...] = jnp.zeros_like(kgrad)
    vgrad[...] = jnp.zeros_like(vgrad)

    def query_block(i, sink_sum):
        at = block_at(i)
        query, cot = recv[0, at, :], recv[3, at, :]
        delta = jnp.sum(cot.astype(f32) * out[0, at, :].astype(f32), axis=1, keepdims=True)
        sink_sum = sink_sum - jnp.sum(sink_share[at, :] * delta, axis=0, keepdims=True)

        def key_step(j, qgrad):
            there = block_at(j)
            keys, values = recv[1, there, :], recv[2, there, :]
            weight = probs[i, j]
            dprob = dot(cot, values, ((1,), (1,)))
            dscore = (weight.astype(f32) * (dprob - delta)).astype(bf16)
            kgrad[there, :] += dot(dscore, query, ((0,), (0,)))
            vgrad[there, :] += dot(weight, cot, ((0,), (0,)))
            return qgrad + dot(dscore, keys)

        qgrad = lax.fori_loop(0, i + 1, key_step, jnp.zeros((BLOCK, width), f32))
        out[1, at, :] = (root * qgrad).astype(bf16)
        return sink_sum

    sink_sum = lax.fori_loop(0, blocks, query_block, jnp.zeros((1, width), f32))

    def round_block(j, carry):
        there = block_at(j)
        out[2, there, :] = (root * kgrad[there, :]).astype(bf16)
        out[3, there, :] = vgrad[there, :].astype(bf16)
        return carry

    lax.fori_loop(0, blocks, round_block, 0)
    return sink_sum


def whole_kernel(
    groups,
    devices,
    ids_ref,
    gate_ref,
    sink_ref,
    q_ref,
    k_ref,
    v_ref,
    og_ref,
    mixed_ref,
    qg_ref,
    kg_ref,
    vg_ref,
    gg_ref,
    sink_out,
    wide,
    og,
    gate_rows,
    gate_sums,
    place_col,
    pick,
    send,
    recv,
    ret,
    back,
    probs,
    strip,
    bias,
    sink_share,
    kgrad,
    vgrad,
    sink_mine,
    sink_all,
    load,
    near,
    sent,
    got,
):
    dp, me = lax.axis_index("dp"), lax.axis_index("head")
    rows, width = q_ref.shape
    tokens, slots, _ = og.shape

    def peers(body):
        def step(n, carry):
            body(lax.rem(me + n, devices))
            return carry

        lax.fori_loop(1, devices, step, 0)

    def group_peers(body):
        def step(n, carry):
            body(lax.rem(dp + n, groups))
            return carry

        lax.fori_loop(1, groups, step, 0)

    loads = [
        pltpu.make_async_copy(ref, wide.at[:, pl.ds(a * width, width)], load.at[a])
        for a, ref in enumerate((q_ref, k_ref, v_ref))
    ] + [pltpu.make_async_copy(og_ref, og, load.at[3])]
    for copy in loads:
        copy.start()
    barrier = pltpu.get_barrier_semaphore()
    peers(lambda d: pl.semaphore_signal(barrier, 1, device_id=(dp, d), device_id_type=MESH))
    group_peers(lambda g: pl.semaphore_signal(barrier, 1, device_id=(g, me), device_id_type=MESH))

    logits = gate_ref[...]
    shifted = jnp.exp(logits - jnp.max(logits, axis=0, keepdims=True))
    gate_rows[...] = (shifted / jnp.sum(shifted, axis=0, keepdims=True)).T
    place = places(ids_ref[...], rows)
    for copy in loads:
        copy.wait()
    cot = gate_rows[...][:, :, None] * og[...].astype(f32)
    wide[:, 3 * width :] = cot.astype(bf16).reshape(rows, width)
    pack(place, wide, send)
    pl.semaphore_wait(barrier, devices - 1 + groups - 1)

    def at(d):
        return pl.ds(pl.multiple_of(d * SLOT, SLOT), SLOT)

    stages = (
        (send, recv, pl.ds(0, 3)),
        (send, recv, pl.ds(3, 1)),
        (ret, back, pl.ds(0, 1)),
        (ret, back, pl.ds(1, 1)),
        (ret, back, pl.ds(2, 1)),
        (ret, back, pl.ds(3, 1)),
    )

    def own(phase):
        source, target, arrays = stages[phase]
        return pltpu.make_async_copy(
            source.at[arrays, at(me)], target.at[arrays, at(me)], near.at[phase]
        )

    def begin(phase):
        source, target, arrays = stages[phase]
        own(phase).start()
        peers(
            lambda d: pltpu.make_async_remote_copy(
                src_ref=source.at[arrays, at(d)],
                dst_ref=target.at[arrays, at(me)],
                send_sem=sent.at[phase],
                recv_sem=got.at[phase],
                device_id=(dp, d),
                device_id_type=MESH,
            ).start()
        )

    def all_of(ref, arrays, sem):
        piece = ref.at[arrays, pl.ds(0, (devices - 1) * SLOT)]
        pltpu.make_async_copy(piece, piece, sem).wait()

    def arrived(phase):
        _, target, arrays = stages[phase]
        own(phase).wait()
        all_of(target, arrays, got.at[phase])

    root = 1.0 / math.sqrt(width)
    begin(0)
    begin(1)
    place_col[...] = jnp.broadcast_to(place, (8, rows)).T

    def pick_block(c, carry):
        slot = iota((BLOCK, HEADS * SLOT), 1)
        pick[block_at(c), :] = one_hot(slot == place_col[block_at(c), 0:1])
        return carry

    lax.fori_loop(0, rows // BLOCK, pick_block, 0)
    arrived(0)
    sink = sink_ref[0] * math.log2(math.e)
    forward(recv, sink, ret, probs, strip, bias, sink_share, root * math.log2(math.e))
    begin(2)
    arrived(1)
    sink_sum = backward(recv, ret, probs, sink_share, kgrad, vgrad, root)
    for phase in (3, 4, 5):
        begin(phase)
    sink_mine[...] = jnp.broadcast_to(sink_sum, sink_mine.shape)
    group_peers(
        lambda g: pltpu.make_async_remote_copy(
            src_ref=sink_mine,
            dst_ref=sink_all.at[dp],
            send_sem=sent.at[6],
            recv_sem=got.at[6],
            device_id=(g, me),
            device_id_type=MESH,
        ).start()
    )
    own_sink = pltpu.make_async_copy(sink_mine, sink_all.at[dp], near.at[6])
    own_sink.start()

    step = BLOCK // slots

    def collect(a, store):
        def chunk(c, carry):
            part = dot(pick[block_at(c), :], back[a])
            store(pl.ds(pl.multiple_of(c * step, step), step), part.reshape(step, slots, width))
            return carry

        lax.fori_loop(0, rows // BLOCK, chunk, 0)

    def store_mixed(here, part):
        mixed_ref[here] = (gate_rows[here][:, :, None] * part).astype(bf16)
        gate_sums[here] = jnp.sum(og[here].astype(f32) * part, axis=-1)

    arrived(2)
    collect(0, store_mixed)
    gate = gate_rows[...]
    gate_sum = gate_sums[...]
    mean = jnp.sum(gate * gate_sum, axis=-1, keepdims=True)
    gg_ref[...] = (gate * (gate_sum - mean)).T
    others = sink_all.at[pl.ds(0, groups - 1)]
    pltpu.make_async_copy(others, others, got.at[6]).wait()
    own_sink.wait()
    sink_out[0] = jnp.sum(jnp.sum(sink_all[...], axis=0)[0:1, 0:1])
    for a, ref in ((1, qg_ref), (2, kg_ref), (3, vg_ref)):
        arrived(a + 2)

        def store(here, part, ref=ref):
            ref[here] = part.astype(bf16)

        collect(a, store)
    for phase, (source, _, arrays) in enumerate(stages):
        all_of(source, arrays, sent.at[phase])
    pltpu.make_async_copy(others, others, sent.at[6]).wait()


def whole(groups, devices, ids, gate_logits, sink_logits, q, k, v, og):
    tokens, slots, width = og.shape
    rows = tokens * slots
    padded = HEADS * SLOT
    blocks = padded // BLOCK
    vmem = pl.BlockSpec(memory_space=pltpu.VMEM)
    smem = pl.BlockSpec(memory_space=pltpu.SMEM)
    hbm = pl.BlockSpec(memory_space=pl.ANY)
    grad = jax.ShapeDtypeStruct((tokens, slots, width), bf16)

    def body(*refs):
        whole_kernel(groups, devices, *refs)

    return pl.pallas_call(
        body,
        out_shape=(grad,) * 4
        + (jax.ShapeDtypeStruct((slots, tokens), f32), jax.ShapeDtypeStruct((1,), f32)),
        in_specs=[vmem, vmem, smem, hbm, hbm, hbm, hbm],
        out_specs=(vmem,) * 5 + (smem,),
        scratch_shapes=[
            pltpu.VMEM((rows, 4 * width), bf16),
            pltpu.VMEM((tokens, slots, width), bf16),
            pltpu.VMEM((tokens, slots), f32),
            pltpu.VMEM((tokens, slots), f32),
            pltpu.VMEM((rows, 8), jnp.int32),
            pltpu.VMEM((rows, padded), bf16),
            pltpu.VMEM((4, padded, width), bf16),
            pltpu.VMEM((4, padded, width), bf16),
            pltpu.VMEM((4, padded, width), bf16),
            pltpu.VMEM((4, padded, width), bf16),
            pltpu.VMEM((blocks, blocks, BLOCK, BLOCK), bf16),
            pltpu.VMEM((blocks, BLOCK, BLOCK), f32),
            pltpu.VMEM((blocks, 8, BLOCK), f32),
            pltpu.VMEM((padded, width), f32),
            pltpu.VMEM((padded, width), f32),
            pltpu.VMEM((padded, width), f32),
            pltpu.VMEM((8, width), f32),
            pltpu.VMEM((groups, 8, width), f32),
            pltpu.SemaphoreType.DMA((4,)),
            pltpu.SemaphoreType.DMA((7,)),
            pltpu.SemaphoreType.DMA((7,)),
            pltpu.SemaphoreType.DMA((7,)),
        ],
        compiler_params=pltpu.CompilerParams(
            collective_id=0, has_side_effects=True, vmem_limit_bytes=60 * 2**20
        ),
    )(
        ids,
        gate_logits,
        sink_logits,
        q.reshape(rows, width),
        k.reshape(rows, width),
        v.reshape(rows, width),
        og,
    )


def per_device(head_ids, query_slots, key_slots, value_slots, gate_logits, sink_logits, out_grad):
    mixed, qgrad, kgrad, vgrad, gate_grad, sink_grad = whole(
        lax.axis_size("dp"),
        lax.axis_size("head"),
        head_ids[0].T,
        gate_logits[0].T,
        sink_logits,
        query_slots[0],
        key_slots[0],
        value_slots[0],
        out_grad[0],
    )
    return mixed[None], qgrad[None], kgrad[None], vgrad[None], gate_grad.T[None], sink_grad


def solution(mesh):
    rows3 = P("dp", "head", None)
    rows4 = P("dp", "head", None, None)
    return jax.shard_map(
        per_device,
        mesh=mesh,
        in_specs=(rows3, rows4, rows4, rows4, rows3, P("head"), rows4),
        out_specs=(rows4, rows4, rows4, rows4, rows3, P("head")),
        check_vma=False,
    )
```

time: 370 us -> 212 us (0.57)
  Pallas kernels: 0 us -> 204 us
  waiting for transfers between devices: 165 us -> 0 us
  starting transfers between devices: 62.6 us -> 0 us
  local copies, waits for them, and re-layouts: 55 us -> 5.1 us
  matrix products: 47.3 us -> 0 us
  other arithmetic: 19.9 us -> 0 us
  blocking collectives: 14.2 us -> 0 us
    pallas_call x0 -> x1, Pallas kernels: none -> 204 us  [whole(): pl.pallas_call(body, out_shape=(grad,) * 4 + (jax.ShapeDtypeStruct((slots...]
    all_to_all x6 -> x0, waiting for transfers between devices: 165 us -> none  [the longest x1 78.5 us: in_one_piece(): lax.all_to_all(both, axis, split_axis=split_dim, concat_axis=concat_dim,...]
    all_to_all x6 -> x0, starting transfers between devices: 62.6 us -> none  [the longest x1 18.8 us: per_device(): lax.all_to_all(filled, 'head', split_axis=0, concat_axis=0, tiled=True)]
    dot_general x70 -> x0, matrix products: 47.3 us -> none  [the longest x10 16.7 us: value_step(): jnp.dot(weights, value_tile, preferred_element_type=jnp.float32)]
    scatter x4 -> x0, local copies, waits for them, and re-layouts: 19.5 us -> none  [the longest x3 12 us: spread_out(): jnp.zeros((buffer_rows, flat_rows.shape[-1]), flat_rows.dtype).at[target]]
    gather x4 -> x0, local copies, waits for them, and re-layouts: 16.1 us -> none  [collect(): buffer.reshape(buffer_rows, buffer.shape[-1])[target]]
    unnamed x1 -> x0, blocking collectives: 14.2 us -> none
    dynamic_slice x54 -> x0, local copies, waits for them, and re-layouts: 7.66 us -> none  [the longest x4 3.94 us: backward_query_block(): cot_tile = lax.dynamic_slice_in_dim(cot_rows, offset, width, 0)]
  transfers between devices with their start and end apart: 6 -> 0, of which waited for: 5 -> 0; matrix products, arithmetic and copies ran while one was open for 14% -> 0% of each run, Pallas kernels for 0% -> 0%
where the time goes in v1:
time: 212 us
  Pallas kernels  204 us (96%)
  local copies, waits for them, and re-layouts  5.1 us (2%)
  between operations  3.05 us (1%)
    pallas_call x1, Pallas kernels, whole(): pl.pallas_call(body, out_shape=(grad,) * 4 + (jax.ShapeDtypeStruct((slots...  204 us
    unnamed x13, local copies, waits for them, and re-layouts  5.1 us

profile of v1, /device:TPU:6, one launch (start us, length us, event | category | flops | bytes accessed | tf_op | source)
XLA Modules:
  0.0 212.1 jit_solution(13130195922021459133)
XLA Ops:
  1.3 204.0 %shard_map.118 = (bf16[128,8,128]{2,1,0:T(8,128)(2,1)}, bf16[128,8,128]{2,1,0:T(8,128)(2,1)}, bf16[128,8,128]{2,1,0:T(8,128)(2,1)}, bf16[128,8,128]{2,1,0:T(8,128)(2,1)}, f32[8,128]{1,0:T(8,128)}, /*index=5*/f32[1]{0:T(128)}) custom-call(s32[8,128]{1,0:T(8,128)} %bitcast.25, f32[8,128]{1,0:T(8,128)} %bitcast.26, f32[1]{0:T(128)S(6)} %copy.19.refs_2_, ...), custom_call_target="tpu_custom_call" | custom-call | tf_op jit(solution)/shard_map/pallas_call | solution.py:370
  205.2 0.0 copy-start.2
  205.2 1.7 copy.20
  207.0 0.0 copy-done.2
  207.0 0.0 copy-start.1
  207.0 0.7 copy.21
  207.7 0.3 copy-done.1
  208.0 0.0 copy-start
  208.0 0.7 copy.22
  208.7 0.3 copy-done
  209.1 0.0 copy-start.3
  209.1 0.7 copy.23
  209.8 0.0 copy-done.3
  209.8 0.6 copy.24
Async XLA Ops:
  205.2 1.7 copy-start.2
  207.0 1.0 copy-start.1
  208.0 1.0 copy-start
  209.1 0.7 copy-start.3

commit v2 on v1

--- a/solution.py
+++ b/solution.py
@@ -169,8 +169,8 @@
 def whole_kernel(
     groups,
     devices,
-    ids_ref,
-    gate_ref,
+    ids_hbm,
+    gate_hbm,
     sink_ref,
     q_ref,
     k_ref,
@@ -182,6 +182,8 @@
     vg_ref,
     gg_ref,
     sink_out,
+    ids_ref,
+    gate_ref,
     wide,
     og,
     gate_rows,
@@ -226,21 +228,29 @@
     loads = [
         pltpu.make_async_copy(ref, wide.at[:, pl.ds(a * width, width)], load.at[a])
         for a, ref in enumerate((q_ref, k_ref, v_ref))
-    ] + [pltpu.make_async_copy(og_ref, og, load.at[3])]
+    ] + [
+        pltpu.make_async_copy(ref, held, load.at[a])
+        for a, ref, held in (
+            (3, og_ref, og),
+            (4, ids_hbm, ids_ref),
+            (5, gate_hbm, gate_ref),
+        )
+    ]
     for copy in loads:
         copy.start()
     barrier = pltpu.get_barrier_semaphore()
     peers(lambda d: pl.semaphore_signal(barrier, 1, device_id=(dp, d), device_id_type=MESH))
     group_peers(lambda g: pl.semaphore_signal(barrier, 1, device_id=(g, me), device_id_type=MESH))
 
+    for copy in loads:
+        copy.wait()
     logits = gate_ref[...]
     shifted = jnp.exp(logits - jnp.max(logits, axis=0, keepdims=True))
     gate_rows[...] = (shifted / jnp.sum(shifted, axis=0, keepdims=True)).T
     place = places(ids_ref[...], rows)
-    for copy in loads:
-        copy.wait()
     cot = gate_rows[...][:, :, None] * og[...].astype(f32)
     wide[:, 3 * width :] = cot.astype(bf16).reshape(rows, width)
+
     pack(place, wide, send)
     pl.semaphore_wait(barrier, devices - 1 + groups - 1)
 
@@ -354,6 +364,10 @@
     pltpu.make_async_copy(others, others, sent.at[6]).wait()
 
 
+def held(array):
+    return pltpu.with_memory_space_constraint(array, pltpu.HBM)
+
+
 def whole(groups, devices, ids, gate_logits, sink_logits, q, k, v, og):
     tokens, slots, width = og.shape
     rows = tokens * slots
@@ -361,7 +375,7 @@
     blocks = padded // BLOCK
     vmem = pl.BlockSpec(memory_space=pltpu.VMEM)
     smem = pl.BlockSpec(memory_space=pltpu.SMEM)
-    hbm = pl.BlockSpec(memory_space=pl.ANY)
+    hbm = pl.BlockSpec(memory_space=pltpu.HBM)
     grad = jax.ShapeDtypeStruct((tokens, slots, width), bf16)
 
     def body(*refs):
@@ -371,9 +385,11 @@
         body,
         out_shape=(grad,) * 4
         + (jax.ShapeDtypeStruct((slots, tokens), f32), jax.ShapeDtypeStruct((1,), f32)),
-        in_specs=[vmem, vmem, smem, hbm, hbm, hbm, hbm],
+        in_specs=[hbm, hbm, smem, hbm, hbm, hbm, hbm],
         out_specs=(vmem,) * 5 + (smem,),
         scratch_shapes=[
+            pltpu.VMEM((slots, tokens), jnp.int32),
+            pltpu.VMEM((slots, tokens), f32),
             pltpu.VMEM((rows, 4 * width), bf16),
             pltpu.VMEM((tokens, slots, width), bf16),
             pltpu.VMEM((tokens, slots), f32),
@@ -392,27 +408,56 @@
             pltpu.VMEM((padded, width), f32),
             pltpu.VMEM((8, width), f32),
             pltpu.VMEM((groups, 8, width), f32),
-            pltpu.SemaphoreType.DMA((4,)),
+            pltpu.SemaphoreType.DMA((6,)),
             pltpu.SemaphoreType.DMA((7,)),
             pltpu.SemaphoreType.DMA((7,)),
             pltpu.SemaphoreType.DMA((7,)),
         ],
         compiler_params=pltpu.CompilerParams(
-            collective_id=0, has_side_effects=True, vmem_limit_bytes=60 * 2**20
+            collective_id=0, has_side_effects=True, vmem_limit_bytes=40 * 2**20
         ),
     )(
-        ids,
-        gate_logits,
+        held(ids),
+        held(gate_logits),
         sink_logits,
-        q.reshape(rows, width),
-        k.reshape(rows, width),
-        v.reshape(rows, width),
-        og,
-    )
+        held(q.reshape(rows, width)),
+        held(k.reshape(rows, width)),
+        held(v.reshape(rows, width)),
+        held(og),
+    )
+
+
+def publish_kernel(count, *refs):
+    sources, targets, done = refs[:count], refs[count : 2 * count], refs[2 * count]
+    copies = [
+        pltpu.make_async_copy(source, target, done.at[n])
+        for n, (source, target) in enumerate(zip(sources, targets))
+    ]
+    for copy in copies:
+        copy.start()
+    for copy in copies:
+        copy.wait()
+
+
+def publish(*arrays):
+    count = len(arrays)
+    places_in = [pl.BlockSpec(memory_space=pltpu.VMEM)] * (count - 1)
+
+    def body(*refs):
+        publish_kernel(count, *refs)
+
+    return pl.pallas_call(
+        body,
+        out_shape=tuple(jax.ShapeDtypeStruct(a.shape, a.dtype) for a in arrays),
+        in_specs=places_in + [pl.BlockSpec(memory_space=pltpu.SMEM)],
+        out_specs=(pl.BlockSpec(memory_space=pltpu.HBM),) * count,
+        scratch_shapes=[pltpu.SemaphoreType.DMA((count,))],
+        compiler_params=pltpu.CompilerParams(vmem_limit_bytes=4 * 2**20),
+    )(*arrays)
 
 
 def per_device(head_ids, query_slots, key_slots, value_slots, gate_logits, sink_logits, out_grad):
-    mixed, qgrad, kgrad, vgrad, gate_grad, sink_grad = whole(
+    results = whole(
         lax.axis_size("dp"),
         lax.axis_size("head"),
         head_ids[0].T,
@@ -423,6 +468,7 @@
         value_slots[0],
         out_grad[0],
     )
+    mixed, qgrad, kgrad, vgrad, gate_grad, sink_grad = publish(*results)
     return mixed[None], qgrad[None], kgrad[None], vgrad[None], gate_grad.T[None], sink_grad
 
 

time: 212 us -> 206 us (0.972)
  local copies, waits for them, and re-layouts: 5.1 us -> 0 us
    unnamed x13 -> x0, local copies, waits for them, and re-layouts: 5.1 us -> none
where the time goes in v2:
time: 206 us
  Pallas kernels  204 us (99%)
    pallas_call x1, Pallas kernels, whole(): pl.pallas_call(body, out_shape=(grad,) * 4 + (jax.ShapeDtypeStruct((slots...  203 us

profile of v2, /device:TPU:6, one launch (start us, length us, event | category | flops | bytes accessed | tf_op | source)
XLA Modules:
  0.0 205.5 jit_solution(12346557178645441433)
XLA Ops:
  1.3 202.6 %shard_map.118 = (bf16[128,8,128]{2,1,0:T(8,128)(2,1)S(1)}, bf16[128,8,128]{2,1,0:T(8,128)(2,1)S(1)}, bf16[128,8,128]{2,1,0:T(8,128)(2,1)S(1)}, bf16[128,8,128]{...) custom-call(s32[8,128]{1,0:T(8,128)} %bitcast.21, f32[8,128]{1,0:T(8,128)} %bitcast.22, f32[1]{0:T(128)S(6)} %copy.13.refs_2_, ...), custom_call_target="tpu_custom_call" | custom-call | tf_op jit(solution)/shard_map/pallas_call | solution.py:384
  203.9 1.7 shard_map.119

commit v3 on v2

--- a/solution.py
+++ b/solution.py
@@ -9,6 +9,7 @@
 
 HEADS = 64
 SLOT = 32
+RING = 16
 DEAD = 2.0**100
 MASKED = -1e30
 BLOCK = 256
@@ -47,23 +48,24 @@
     return jnp.sum(jnp.where(mine, place, 0.0), axis=0, keepdims=True).astype(jnp.int32)
 
 
-def pack(place, wide, send):
+def pack(place, wide, send, first, last):
     rows, width = wide.shape[0], wide.shape[1] // 4
     ones = jnp.ones((rows, width), bf16)
+    size = 2 * BLOCK
 
     def chunk(c, carry):
-        slot = c * BLOCK + iota((BLOCK, rows), 0)
+        slot = c * size + iota((size, rows), 0)
         pick = one_hot(slot == place)
-        moved = dot(pick, wide[...])
-        live = dot(pick, ones)
-        for a in range(4):
-            part = moved[:, a * width : (a + 1) * width]
+        moved = dot(pick, wide[:, first * width : last * width])
+        for a in range(first, last):
+            part = moved[:, (a - first) * width : (a - first + 1) * width]
             if a == 1:
-                part = jnp.where((live < 0.5) & (iota((BLOCK, width), 1) == 0), DEAD, part)
-            send[a, block_at(c), :] = part.astype(bf16)
-        return carry
-
-    lax.fori_loop(0, send.shape[1] // BLOCK, chunk, 0)
+                live = dot(pick, ones)
+                part = jnp.where((live < 0.5) & (iota((size, width), 1) == 0), DEAD, part)
+            send[a, pl.ds(pl.multiple_of(c * size, size), size), :] = part.astype(bf16)
+        return carry
+
+    lax.fori_loop(0, send.shape[1] // size, chunk, 0)
 
 
 def forward(recv, sink, out, probs, strip, bias, sink_share, factor):
@@ -239,19 +241,24 @@
     for copy in loads:
         copy.start()
     barrier = pltpu.get_barrier_semaphore()
-    peers(lambda d: pl.semaphore_signal(barrier, 1, device_id=(dp, d), device_id_type=MESH))
+    lines = devices // RING
+
+    def greet(n, carry):
+        d = lax.rem(n, lines) * RING + n // lines
+
+        @pl.when(d != me)
+        def _():
+            pl.semaphore_signal(barrier, 1, device_id=(dp, d), device_id_type=MESH)
+
+        return carry
+
+    lax.fori_loop(0, devices, greet, 0)
     group_peers(lambda g: pl.semaphore_signal(barrier, 1, device_id=(g, me), device_id_type=MESH))
 
     for copy in loads:
         copy.wait()
-    logits = gate_ref[...]
-    shifted = jnp.exp(logits - jnp.max(logits, axis=0, keepdims=True))
-    gate_rows[...] = (shifted / jnp.sum(shifted, axis=0, keepdims=True)).T
     place = places(ids_ref[...], rows)
-    cot = gate_rows[...][:, :, None] * og[...].astype(f32)
-    wide[:, 3 * width :] = cot.astype(bf16).reshape(rows, width)
-
-    pack(place, wide, send)
+    pack(place, wide, send, 0, 3)
     pl.semaphore_wait(barrier, devices - 1 + groups - 1)
 
     def at(d):
@@ -297,6 +304,13 @@
 
     root = 1.0 / math.sqrt(width)
     begin(0)
+    logits = gate_ref[...]
+    shifted = jnp.exp(logits - jnp.max(logits, axis=0, keepdims=True))
+    gate_rows[...] = (shifted / jnp.sum(shifted, axis=0, keepdims=True)).T
+    cot = gate_rows[...][:, :, None] * og[...].astype(f32)
+    wide[:, 3 * width :] = cot.astype(bf16).reshape(rows, width)
+
+    pack(place, wide, send, 3, 4)
     begin(1)
     place_col[...] = jnp.broadcast_to(place, (8, rows)).T
 

time: 206 us -> 207 us (level)
  no operation moved by 1% of the time
where the time goes in v3:
time: 207 us; the launch traced here: 206 us
  Pallas kernels  204 us (99%)
    pallas_call x1, Pallas kernels, whole(): pl.pallas_call(body, out_shape=(grad,) * 4 + (jax.ShapeDtypeStruct((slots...  203 us

profile of v3, /device:TPU:6, one launch (start us, length us, event | category | flops | bytes accessed | tf_op | source)
XLA Modules:
  0.0 205.8 jit_solution(15376022228582386978)
XLA Ops:
  1.3 202.8 %shard_map.118 = (bf16[128,8,128]{2,1,0:T(8,128)(2,1)S(1)}, bf16[128,8,128]{2,1,0:T(8,128)(2,1)S(1)}, bf16[128,8,128]{2,1,0:T(8,128)(2,1)S(1)}, bf16[128,8,128]{...) custom-call(s32[8,128]{1,0:T(8,128)} %bitcast.21, f32[8,128]{1,0:T(8,128)} %bitcast.22, f32[1]{0:T(128)S(6)} %copy.13.refs_2_, ...), custom_call_target="tpu_custom_call" | custom-call | tf_op jit(solution)/shard_map/pallas_call | solution.py:398
  204.1 1.7 shard_map.119
